TPU v7x, 32 devices: a whole 2x2x4 slice. The times are simulated.
32 devices in a mesh: batch: 32 (over z, y, x, core).
Axes of the slice: x: 2, y: 2, z: 4, core: 2. Of those that a mesh axis runs over, the one named last changes fastest.
Arguments:
- tokens: bfloat16 [32768, 768], P('batch'), may hold values from -6 to 6
- segment_ids: int32 [64, 512], P('batch'), may hold values from -1 to 7, as said below
- pair_index: int32 [512], P('batch'), may hold values from 0 to 511, as said below
- qkv_weight: bfloat16 [768, 2304], replicated, may hold values from -0.21875 to 0.21875
- query_bias: float32 [768], replicated, may hold values from -1.75 to 1.75
- value_bias: float32 [768], replicated, may hold values from -1.75 to 1.75
- proj_weight: bfloat16 [768, 768], replicated, may hold values from -0.875 to 0.875
- proj_bias: float32 [768], replicated, may hold values from -1.75 to 1.75
- attn_gain: float32 [768], replicated, may hold values from 0.5 to 1.5
- attn_shift: float32 [768], replicated, may hold values from -1.75 to 1.75
- up_weight: bfloat16 [768, 3072], replicated, may hold values from -0.21875 to 0.21875
- up_bias: float32 [3072], replicated, may hold values from -1.75 to 1.75
- down_weight: bfloat16 [3072, 768], replicated, may hold values from -0.109375 to 0.109375
- down_bias: float32 [768], replicated, may hold values from -1.75 to 1.75
- ffn_gain: float32 [768], replicated, may hold values from 0.5 to 1.5
- ffn_shift: float32 [768], replicated, may hold values from -1.75 to 1.75
Outputs:
- loss: float32 [], replicated
- layer_out: bfloat16 [32768, 768], P('batch')
- tokens_grad: float32 [32768, 768], P('batch')
- qkv_weight_grad: float32 [1769472], P('batch')
- proj_weight_grad: float32 [589824], P('batch')
- up_weight_grad: float32 [2359296], P('batch')
- down_weight_grad: float32 [2359296], P('batch')
- query_bias_grad: float32 [768], replicated
- value_bias_grad: float32 [768], replicated
- proj_bias_grad: float32 [768], replicated
- attn_gain_grad: float32 [768], replicated
- attn_shift_grad: float32 [768], replicated
- up_bias_grad: float32 [3072], replicated
- down_bias_grad: float32 [768], replicated
- ffn_gain_grad: float32 [768], replicated
- ffn_shift_grad: float32 [768], replicated
Inputs may be any that keep to these rules, and one draw needn't show every extreme that they name: `segment_ids`: each row holds segments 0 to 7 in this order, each of one or more tokens, followed by eight or more padding tokens of -1. `pair_index`: each segment is the positive of exactly one query and no query is its own positive.
All inputs are finite; a program needn't handle non-finite values.
Results may differ from a plain program's by a relative error of at most 0.012.
Values may be sent and summed in bfloat16 or wider, within the bound.
A program may use at most 192 MiB of HBM per device.

v0:
```python
import jax
import jax.numpy as jnp
from jax import lax
from jax.sharding import PartitionSpec as P

HEADS = 12
HEAD_DIM = 64
SEGS = 8


inv_temp = 100.0
ln_eps = 1e-12
norm_eps = 1e-06
neg_fill = -1000000000.0


def flat_dot(left, right):
    return jnp.dot(left, right, preferred_element_type=jnp.float32)


def trans_dot(left, right):
    return lax.dot_general(
        left, right, (((0,), (0,)), ((), ())), preferred_element_type=jnp.float32
    )


def back_dot(left, right):
    return lax.dot_general(
        left, right, (((1,), (1,)), ((), ())), preferred_element_type=jnp.float32
    )


def normalize(resid):
    average = jnp.mean(resid, axis=-1, keepdims=True)
    centred = resid - average
    variance = jnp.mean(centred * centred, axis=-1, keepdims=True)
    inv_std = lax.rsqrt(variance + ln_eps)
    return (centred * inv_std, inv_std)


def norm_back(grad_out, normed, inv_std, gain):
    grad_n = grad_out * gain
    return inv_std * (
        grad_n
        - jnp.mean(grad_n, axis=-1, keepdims=True)
        - normed * jnp.mean(grad_n * normed, axis=-1, keepdims=True)
    )


def row_scores(qkv_row, ids_row):
    split_qkv = qkv_row.reshape(qkv_row.shape[0], 3, HEADS, HEAD_DIM)
    queries, key_vecs, values = (split_qkv[:, 0], split_qkv[:, 1], split_qkv[:, 2])
    raw_scores = jnp.einsum(
        "qhd,khd->hqk", queries, key_vecs, preferred_element_type=jnp.float32
    ) * HEAD_DIM ** (-0.5)
    same_segment = ids_row[:, None] == ids_row[None, :]
    return (jnp.where(same_segment[None], raw_scores, neg_fill), queries, key_vecs, values)


def attend_row(entry):
    qkv_row, ids_row = entry
    masked, queries, key_vecs, values = row_scores(qkv_row, ids_row)
    peak_val = jnp.max(masked, axis=-1, keepdims=True)
    exponent = jnp.exp(masked - peak_val)
    denom_sum = jnp.sum(exponent, axis=-1, keepdims=True)
    probs_low = (exponent / denom_sum).astype(jnp.bfloat16)
    context = jnp.einsum("hqk,khd->qhd", probs_low, values, preferred_element_type=jnp.float32)
    log_total = peak_val[..., 0] + jnp.log(denom_sum[..., 0])
    return (context.reshape(qkv_row.shape[0], HEADS * HEAD_DIM).astype(jnp.bfloat16), log_total)


def attend_back(entry):
    qkv_row, ids_row, log_total, grad_row = entry
    masked, queries, key_vecs, values = row_scores(qkv_row, ids_row)
    attn_probs = jnp.exp(masked - log_total[..., None])
    probs_low = attn_probs.astype(jnp.bfloat16)
    grad_ctx = grad_row.reshape(qkv_row.shape[0], HEADS, HEAD_DIM)
    grad_probs = jnp.einsum("qhd,khd->hqk", grad_ctx, values, preferred_element_type=jnp.float32)
    grad_values = jnp.einsum(
        "hqk,qhd->khd", probs_low, grad_ctx, preferred_element_type=jnp.float32
    )
    row_delta = jnp.sum(attn_probs * grad_probs, axis=-1, keepdims=True)
    grad_scores = (attn_probs * (grad_probs - row_delta)).astype(jnp.bfloat16)
    grad_queries = jnp.einsum(
        "hqk,khd->qhd", grad_scores, key_vecs, preferred_element_type=jnp.float32
    ) * HEAD_DIM ** (-0.5)
    grad_keys = jnp.einsum(
        "hqk,qhd->khd", grad_scores, queries, preferred_element_type=jnp.float32
    ) * HEAD_DIM ** (-0.5)
    stacked = jnp.stack([grad_queries, grad_keys, grad_values], axis=1)
    return stacked.reshape(qkv_row.shape[0], 3 * HEADS * HEAD_DIM).astype(jnp.bfloat16)


def per_device(
    tokens,
    segment_ids,
    pair_index,
    qkv_weight,
    query_bias,
    value_bias,
    proj_weight,
    proj_bias,
    attn_gain,
    attn_shift,
    up_weight,
    up_bias,
    down_weight,
    down_bias,
    ffn_gain,
    ffn_shift,
):
    rows_here = segment_ids.shape[0]
    row_len = segment_ids.shape[1]
    tok_here = tokens.shape[0]
    seg_here = pair_index.shape[0]
    width = tokens.shape[1]
    total_seg = seg_here * lax.axis_size("batch")
    own_rows = lax.axis_index("batch") * seg_here + jnp.arange(seg_here, dtype=jnp.int32)
    x_float = tokens.astype(jnp.float32)
    bias_full = jnp.concatenate([query_bias, jnp.zeros_like(query_bias), value_bias])
    qkv_all = (flat_dot(tokens, qkv_weight) + bias_full).astype(jnp.bfloat16)
    qkv_rows = qkv_all.reshape(rows_here, row_len, 3 * width)
    context, log_rows = lax.map(attend_row, (qkv_rows, segment_ids))
    context = context.reshape(tok_here, width)
    attended = flat_dot(context, proj_weight) + proj_bias
    normed_one, inv_one = normalize(x_float + attended)
    first_norm = normed_one * attn_gain + attn_shift
    first_low = first_norm.astype(jnp.bfloat16)
    up_pre = flat_dot(first_low, up_weight) + up_bias
    acted = jax.nn.gelu(up_pre, approximate=False).astype(jnp.bfloat16)
    down_out = flat_dot(acted, down_weight) + down_bias
    normed_two, inv_two = normalize(first_norm + down_out)
    outputs = normed_two * ffn_gain + ffn_shift
    row_base = (jnp.arange(rows_here, dtype=jnp.int32) * SEGS)[:, None]
    local_ids = jnp.where(segment_ids >= 0, segment_ids + row_base, -1).reshape(tok_here)
    member = (local_ids[None, :] == jnp.arange(seg_here, dtype=jnp.int32)[:, None]).astype(
        jnp.float32
    )
    counts = jnp.sum(member, axis=1, keepdims=True)
    pooled = jnp.dot(member, outputs, precision=lax.Precision.HIGHEST) / counts
    inv_norm = lax.rsqrt(jnp.sum(pooled * pooled, axis=1, keepdims=True) + norm_eps)
    embedding = pooled * inv_norm
    embed_low = embedding.astype(jnp.bfloat16)

    def block_scores(shard_piece):
        raw_scores = back_dot(embed_low, shard_piece) * inv_temp
        columns = jnp.arange(shard_piece.shape[0], dtype=jnp.int32)
        masked = jnp.where(columns[None, :] == own_rows[:, None], neg_fill, raw_scores)
        positive_mask = columns[None, :] == pair_index[:, None]
        return (raw_scores, masked, positive_mask)

    start_peak = jnp.full((seg_here,), -1e30, jnp.float32)
    peak_val = start_peak
    raw_scores, masked, positive_mask = block_scores(
        lax.all_gather(embed_low, "batch", axis=0, tiled=True)
    )
    new_peak = jnp.maximum(peak_val, jnp.max(masked, axis=1))
    denom_sum = jnp.sum(jnp.exp(masked - new_peak[:, None]), axis=1)
    positive = jnp.sum(jnp.where(positive_mask, raw_scores, 0.0), axis=1)
    peak_val, denom_sum, positive = (new_peak, denom_sum, positive)
    log_norm = peak_val + jnp.log(denom_sum)
    shard_piece = lax.all_gather(embed_low, "batch", axis=0, tiled=True)
    raw_scores, masked, positive_mask = block_scores(shard_piece)
    weights_low = (jnp.exp(masked - log_norm[:, None]) - positive_mask.astype(jnp.float32)).astype(
        jnp.bfloat16
    )
    grad_acc = flat_dot(weights_low, shard_piece) * inv_temp
    loss_value = lax.psum(jnp.sum(log_norm - positive), "batch") / total_seg
    grad_passage = lax.psum_scatter(
        trans_dot(weights_low, embed_low) * inv_temp, "batch", scatter_dimension=0, tiled=True
    )
    grad_embed = grad_acc + grad_passage
    grad_pooled = inv_norm * (
        grad_embed - embedding * jnp.sum(grad_embed * embedding, axis=1, keepdims=True)
    )
    grad_y = lax.dot_general(
        member, grad_pooled / counts, (((0,), (0,)), ((), ())), precision=lax.Precision.HIGHEST
    )
    ffn_gain_part = jnp.sum(grad_y * normed_two, axis=0)
    ffn_shift_part = jnp.sum(grad_y, axis=0)
    grad_r2 = norm_back(grad_y, normed_two, inv_two, ffn_gain)
    grad_down_low = grad_r2.astype(jnp.bfloat16)
    down_bias_part = jnp.sum(grad_down_low.astype(jnp.float32), axis=0)
    down_weight_part = trans_dot(acted, grad_down_low)
    grad_acted = back_dot(grad_down_low, down_weight)
    normal_cdf = 0.5 * (1.0 + lax.erf(up_pre * 0.7071067811865476))
    normal_pdf = jnp.exp(-0.5 * up_pre * up_pre) * 0.3989422804014327
    grad_up_low = (grad_acted * (normal_cdf + up_pre * normal_pdf)).astype(jnp.bfloat16)
    up_bias_part = jnp.sum(grad_up_low.astype(jnp.float32), axis=0)
    up_weight_part = trans_dot(first_low, grad_up_low)
    grad_first = grad_r2 + back_dot(grad_up_low, up_weight)
    attn_gain_part = jnp.sum(grad_first * normed_one, axis=0)
    attn_shift_part = jnp.sum(grad_first, axis=0)
    grad_r1 = norm_back(grad_first, normed_one, inv_one, attn_gain)
    grad_att_low = grad_r1.astype(jnp.bfloat16)
    proj_bias_part = jnp.sum(grad_att_low.astype(jnp.float32), axis=0)
    proj_weight_part = trans_dot(context, grad_att_low)
    grad_context = back_dot(grad_att_low, proj_weight).astype(jnp.bfloat16)
    grad_qkv = lax.map(
        attend_back,
        (qkv_rows, segment_ids, log_rows, grad_context.reshape(rows_here, row_len, width)),
    )
    grad_qkv = grad_qkv.reshape(tok_here, 3 * width)
    qkv_bias_part = jnp.sum(grad_qkv.astype(jnp.float32), axis=0)
    qkv_weight_part = trans_dot(tokens, grad_qkv)
    tokens_grad = grad_r1 + back_dot(grad_qkv, qkv_weight)
    qkv_weight_grad, proj_weight_grad, up_weight_grad, down_weight_grad = (
        lax.psum_scatter(qkv_weight_part.reshape(-1), "batch", scatter_dimension=0, tiled=True),
        lax.psum_scatter(proj_weight_part.reshape(-1), "batch", scatter_dimension=0, tiled=True),
        lax.psum_scatter(up_weight_part.reshape(-1), "batch", scatter_dimension=0, tiled=True),
        lax.psum_scatter(down_weight_part.reshape(-1), "batch", scatter_dimension=0, tiled=True),
    )
    vector_sums = lax.psum(
        (
            qkv_bias_part[:width],
            qkv_bias_part[2 * width :],
            proj_bias_part,
            attn_gain_part,
            attn_shift_part,
            up_bias_part,
            down_bias_part,
            ffn_gain_part,
            ffn_shift_part,
        ),
        "batch",
    )
    return (
        loss_value,
        outputs.astype(jnp.bfloat16),
        tokens_grad,
        qkv_weight_grad,
        proj_weight_grad,
        up_weight_grad,
        down_weight_grad,
        vector_sums[0],
        vector_sums[1],
        vector_sums[2],
        vector_sums[3],
        vector_sums[4],
        vector_sums[5],
        vector_sums[6],
        vector_sums[7],
        vector_sums[8],
    )


def solution(mesh):
    return jax.shard_map(
        per_device,
        mesh=mesh,
        in_specs=(
            P("batch", None),
            P("batch", None),
            P("batch"),
            P(),
            P(),
            P(),
            P(),
            P(),
            P(),
            P(),
            P(),
            P(),
            P(),
            P(),
            P(),
            P(),
        ),
        out_specs=(
            P(),
            P("batch", None),
            P("batch", None),
            P("batch"),
            P("batch"),
            P("batch"),
            P("batch"),
            P(),
            P(),
            P(),
            P(),
            P(),
            P(),
            P(),
            P(),
            P(),
        ),
        check_vma=False,
    )
```

profile of v0, /device:TPU:0, one launch (start us, length us, event | category | flops | bytes accessed | tf_op | source)
XLA Modules:
  0.0 921.9 jit_solution(3875069064711586793)
XLA Ops:
  7.8 2.9 copy.87
  11.4 7.5 add_convert_fusion
  18.9 6.7 copy.88
  25.6 36.7 %while.22 = (s32[]{:T(128)}, bf16[2,512,768]{2,1,0:T(8,128)(2,1)}, f32[2,12,512]{2,1,0:T(8,128)}, bf16[2,512,2304]{1,2,0:T(8,128)(2,1)}, s32[2,512]{1,0:T(2,128)S(1)}, /*index=5*/s32[]{:T(128)}) while((s32[]{:T(128)}, bf16[2,512,768]{2,1,0:T(8,128)(2,1)}, f32[2,12,512]{2,1,0:T(8,128)}, bf16[2,512,2304]{1,2,0:T(8,128)(2,1)}, ...), condition=%wide.region_3.4_spmd, body=%wide.region_0.3_spmd.sunk | while | flops 843704320 | bytes 60505220 | solution.py:123
  29.9 3.5 fusion.114
  34.1 5.5 fusion.115
  48.3 3.5 fusion.114
  52.4 5.5 fusion.115
  62.3 4.0 fusion.72
  66.8 46.9 %fusion.25 = (bf16[1024,3072]{1,0:T(8,128)(2,1)S(1)}, f32[1024,3072]{1,0:T(8,128)}) fusion(f32[3072]{0:T(1024)S(1)} %copy-done.41, bf16[768,3072]{1,0:T(8,128)(2,1)S(1)} %copy-done.38, f32[1024,768]{0,1:T(8,128)S(1)} %get-tuple-element.246, f32[768]{0:T(1024)S(1)} %copy-done.45, f32[768]{0:T(1024)S(1)} %copy-done.34, f32[1024]{0:T(1024)S(1)} %add_rsqrt_fusion.1, ...), kind=kOutput, calls=%fused_computation.48 | convolution fusion | flops 5043388416 | bytes 26765312 | tf_op jit(solution)/shard_map/dot_general | solution.py:18
  113.8 6.0 fusion.73
  124.9 48.1 %all_gather.4 = bf16[512,768]{1,0:T(8,128)(2,1)} all-gather(bf16[16,768]{1,0:T(8,128)(2,1)S(1)} %multiply_convert_fusion.3), channel_id=1, replica_groups=mesh['batch'=32] {'batch'}, dimensions={0}, use_global_device_ids=true | all-gather | bytes 811008 | tf_op jit(solution)/shard_map/all_gather | solution.py:155
  176.7 2.4 convolution_multiply_fusion
  179.2 93.2 %reduce-scatter.2.cloned.1.call-done = f32[16,768]{1,0:T(8,128)} async-done(((f32[512,768]{1,0:T(8,128)}), f32[16,768]{1,0:T(8,128)}) %reduce-scatter.2.cloned.1.call-update) | async-done | bytes 49168 | tf_op jit(solution)/shard_map/reduce_scatter | solution.py:169
  274.0 4.5 fusion.74
  278.5 3.7 copy.91
  282.2 4.6 multiply_reduce_fusion.1
  286.9 3.1 convert_reduce_fusion.2
  290.0 10.5 %fusion.65 = f32[3072,768]{1,0:T(8,128)} fusion(bf16[1024,3072]{1,0:T(8,128)(2,1)} %copy-done.47, f32[1024,768]{0,1:T(8,128)S(1)} %get-tuple-element.233), kind=kOutput, calls=%fused_computation.151 | convolution fusion | flops 4832624640 | bytes 18874368 | tf_op jit(solution)/shard_map/dot_general | solution.py:22
  300.6 13.8 %convert_reduce_fusion = (f32[3072]{0:T(1024)}, bf16[1024,3072]{1,0:T(8,128)(2,1)}) fusion(f32[1024,3072]{1,0:T(8,128)} %get-tuple-element.248, f32[3072]{0:T(1024)S(1)} %copy-done.42, bf16[3072,768]{1,0:T(8,128)(2,1)S(1)} %bitcast.162, f32[1024,768]{0,1:T(8,128)S(1)} %get-tuple-element.233), kind=kOutput, calls=%fused_computation.55 | convolution fusion | flops 4873516032 | bytes 26763264 | tf_op jit(solution)/shard_map/dot_general | solution.py:28
  314.4 7.5 convolution_bitcast_fusion.1
  321.9 9.1 multiply_reduce_fusion.2
  332.8 2.6 convolution_convert_fusion
  335.4 2.8 fusion.62
  338.2 5.7 copy.112
  343.9 10.8 %reshape.257 = f32[2359296]{0:T(1024)} reshape(f32[3072,768]{1,0:T(8,128)} %fusion.65) | data formatting | bytes 18874368 | tf_op jit(solution)/shard_map/reshape | solution.py:211
  354.7 84.3 %while.23 = (s32[]{:T(128)}, bf16[2,512,2304]{1,2,0:T(8,128)(2,1)}, bf16[2,512,2304]{1,2,0:T(8,128)(2,1)}, s32[2,512]{1,0:T(2,128)S(1)}, f32[2,12,512]{2,1,0:T(8,128)}, /*index=5*/bf16[2,512,768]{2,1,0:T(8,128)(2,1)}, s32[]{:T(128)}) while((s32[]{:T(128)}, bf16[2,512,2304]{1,2,0:T(8,128)(2,1)}, bf16[2,512,2304]{1,2,0:T(8,128)(2,1)}, ...), condition=%wide.region_23.24_spmd, body=%wide.region_21.23_spmd.sunk | while | flops 2065033216 | bytes 188177264 | solution.py:199
  356.9 6.3 fusion.121
  365.8 2.3 copy.116
  368.1 13.6 %multiply_reduce_fusion.12 = (f32[12,512]{1,0:T(8,128)S(1)}, f32[12,512,512]{1,2,0:T(8,128)}) fusion(f32[12,512,512]{1,2,0:T(8,128)} %fusion.121, f32[12,512]{1,0:T(8,128)} %dynamic-slice_bitcast_fusion.2, pred[512,512]{0,1:T(8,128)(4,1)} %broadcast_compare_fusion.5, bf16[512,12,64]{0,2,1:T(8,128)(2,1)} %bitcast.146, ...), kind=kOutput, calls=%fused_computation.19.clone.1 | convolution fusion | flops 418375680 | bytes 27058176 | tf_op jit(solution)/shard_map/while/body/eval_jaxpr/qhd,khd->hqk/dot_general | solution.py:78
  381.7 7.1 multiply_convert_fusion.5
  392.0 3.2 fusion.122
  398.9 6.3 fusion.121
  407.7 2.3 copy.116
  410.0 13.6 %multiply_reduce_fusion.12 = (f32[12,512]{1,0:T(8,128)S(1)}, f32[12,512,512]{1,2,0:T(8,128)}) fusion(f32[12,512,512]{1,2,0:T(8,128)} %fusion.121, f32[12,512]{1,0:T(8,128)} %dynamic-slice_bitcast_fusion.2, pred[512,512]{0,1:T(8,128)(4,1)} %broadcast_compare_fusion.5, bf16[512,12,64]{0,2,1:T(8,128)(2,1)} %bitcast.146, ...), kind=kOutput, calls=%fused_computation.19.clone.1 | convolution fusion | flops 418375680 | bytes 27058176 | tf_op jit(solution)/shard_map/while/body/eval_jaxpr/qhd,khd->hqk/dot_general | solution.py:78
  423.7 7.1 multiply_convert_fusion.5
  434.0 3.2 fusion.122
  439.0 6.9 copy.95
  445.9 9.6 %convolution_bitcast_fusion = f32[768,2304]{0,1:T(8,128)} fusion(bf16[1024,2304]{1,0:T(8,128)(2,1)} %bitcast.151, bf16[1024,768]{1,0:T(8,128)(2,1)} %param.20), kind=kOutput, calls=%fused_computation.73 | convolution fusion | flops 3623878656 | bytes 13369344 | tf_op jit(solution)/shard_map/dot_general | solution.py:22
  455.5 8.1 copy.97
  463.6 7.9 reshape.254
  471.5 3.2 reshape.255
  474.8 3.0 convert_reduce_fusion.1
  478.5 43.9 %all-reduce.4 = (f32[]{:T(128)}, f32[768]{0:T(1024)}, f32[768]{0:T(1024)}, f32[768]{0:T(1024)}, f32[768]{0:T(1024)}, /*index=5*/f32[768]{0:T(1024)}, f32[3072]{0...) all-reduce(f32[]{:T(128)} %get-tuple-element.236, ...), channel_id=1, replica_groups=mesh['batch'=32] {'batch'}, use_global_device_ids=true, to_apply=%region_14.15 | all-reduce | flops 9217 | bytes 73736 | tf_op jit(solution)/shard_map/psum | solution.py:168
  522.4 8.4 convolution_add_fusion.1
  530.8 3.6 copy.100
  534.4 2.6 copy.99
  537.6 369.6 %all-reduce.8.cloned.1.call-done = (f32[1769472]{0:T(1024)}, f32[589824]{0:T(1024)}, f32[2359296]{0:T(1024)}, f32[2359296]{0:T(1024)}) async-done(((f32[1769472]{0:T(1024)}, f32[589824]{0:T(1024)}, f32[2359296]{0:T(1024)}, f32[2359296]{0:T(1024)}), (f32[1769472]{0:T(1024)}, f32[589824]{0:T(1024)}, f32[2359296]{0:T(1024)}, f32[2359296]{0:T(1024)})) %all-reduce.8.cloned.1.call-update) | async-done | bytes 28311568
  (212 shorter events, 58.3 us)
Async XLA Ops:
  7.2 265.2 %reduce-scatter.2.cloned.1.call-start = ((), (), s32[]{:S(2)}) async-start(), calls=%async_computation.1 | async-start | bytes 1622016 | tf_op jit(solution)/shard_map/reduce_scatter | solution.py:169
  18.9 6.7 copy-start.19
  25.6 36.7 %copy-start.43 = (f32[768]{0:T(1024)S(1)}, f32[768]{0:T(1024)}, u32[]{:S(2)}) copy-start(f32[768]{0:T(1024)} %param.27) | copy-start | bytes 9220
  62.3 4.5 copy-start.34
  62.3 4.5 copy-start.38
  62.3 4.5 copy-start.41
  62.3 4.5 copy-start.45
  62.3 51.5 %slice-start.3 = ((s8[4718592]{0:T(1024)(128)(4,1)}), s8[4194304]{0:T(1024)(128)(4,1)S(1)}, s32[]{:S(2)}) async-start(s8[4718592]{0:T(1024)(128)(4,1)} %bitcast.159), calls=%async_computation.6 | async-start | bytes 8388608
  66.3 47.4 %copy-start.10 = (f32[1024,768]{0,1:T(8,128)}, f32[1024,768]{0,1:T(8,128)S(1)}, u32[]{:S(2)}) copy-start(f32[1024,768]{0,1:T(8,128)S(1)} %get-tuple-element.246) | copy-start | bytes 9437188
  66.8 46.9 %copy-start.27 = (f32[1024]{0:T(1024)}, f32[1024]{0:T(1024)S(1)}, u32[]{:S(2)}) copy-start(f32[1024]{0:T(1024)S(1)} %add_rsqrt_fusion.1) | copy-start | bytes 12292
  66.8 46.9 %slice-start.4 = ((s8[4718592]{0:T(1024)(128)(4,1)}), s8[524288]{0:T(1024)(128)(4,1)S(1)}, s32[]{:S(2)}) async-start(s8[4718592]{0:T(1024)(128)(4,1)} %bitcast.159), calls=%async_computation.7 | async-start | bytes 1048576
  66.8 46.9 %copy-start.44 = (f32[768]{0:T(1024)S(1)}, f32[768]{0:T(1024)}, u32[]{:S(2)}) copy-start(f32[768]{0:T(1024)} %param.33) | copy-start | bytes 9220
  113.7 6.1 copy-start.47
  113.8 6.5 copy-start.37
  113.8 7.7 copy-start.21
  113.8 7.7 copy-start.32
  179.1 728.1 %all-reduce.8.cloned.1.call-start = ((), (), s32[]{:S(2)}) async-start(), calls=%async_computation.2 | async-start | bytes 56623104
  282.2 4.6 copy-start.8
  282.2 4.7 copy-start.9
  282.2 4.7 copy-start.22
  282.2 4.7 copy-start.33
  286.9 13.6 %slice-start.5 = ((s8[4718592]{0:T(1024)(128)(4,1)}), s8[4194304]{0:T(1024)(128)(4,1)S(1)}, s32[]{:S(2)}) async-start(s8[4718592]{0:T(1024)(128)(4,1)} %bitcast.161), calls=%async_computation.8 | async-start | bytes 8388608
  290.0 10.5 %slice-start.6 = ((s8[4718592]{0:T(1024)(128)(4,1)}), s8[524288]{0:T(1024)(128)(4,1)S(1)}, s32[]{:S(2)}) async-start(s8[4718592]{0:T(1024)(128)(4,1)} %bitcast.161), calls=%async_computation.9 | async-start | bytes 1048576
  290.0 10.5 %copy-start.42 = (f32[3072]{0:T(1024)S(1)}, f32[3072]{0:T(1024)}, u32[]{:S(2)}) copy-start(f32[3072]{0:T(1024)} %param.31) | copy-start | bytes 36868
  290.0 31.9 %slice-start.7 = ((s8[4718592]{0:T(1024)(128)(4,1)}), s8[4194304]{0:T(1024)(128)(4,1)S(1)}, s32[]{:S(2)}) async-start(s8[4718592]{0:T(1024)(128)(4,1)} %bitcast.163), calls=%async_computation.10 | async-start | bytes 8388608
  300.5 13.9 %copy-start.11 = (f32[1024,768]{0,1:T(8,128)S(1)}, f32[1024,768]{0,1:T(8,128)}, u32[]{:S(2)}) copy-start(f32[1024,768]{0,1:T(8,128)} %copy-done.10) | copy-start | bytes 9437188
  300.5 13.9 %copy-start.28 = (f32[1024]{0:T(1024)S(1)}, f32[1024]{0:T(1024)}, u32[]{:S(2)}) copy-start(f32[1024]{0:T(1024)} %copy-done.27) | copy-start | bytes 12292
  300.6 13.8 %copy-start.35 = (f32[768]{0:T(1024)S(1)}, f32[768]{0:T(1024)}, u32[]{:S(2)}) copy-start(f32[768]{0:T(1024)} %param.28) | copy-start | bytes 9220
  300.6 13.8 %copy-start.46 = (f32[768]{0:T(1024)S(1)}, f32[768]{0:T(1024)}, u32[]{:S(2)}) copy-start(f32[768]{0:T(1024)} %param.29) | copy-start | bytes 9220
  300.6 21.3 %slice-start.8 = ((s8[4718592]{0:T(1024)(128)(4,1)}), s8[524288]{0:T(1024)(128)(4,1)S(1)}, s32[]{:S(2)}) async-start(s8[4718592]{0:T(1024)(128)(4,1)} %bitcast.163), calls=%async_computation.11 | async-start | bytes 1048576
  356.9 6.4 copy-start.1
  356.9 7.3 copy-start.17
  356.9 7.9 copy-start.12
  368.1 13.6 %slice-start = ((s8[12582912]{0:T(1024)(128)(4,1)}), s8[4194304]{0:T(1024)(128)(4,1)S(1)}, s32[]{:S(2)}) async-start(s8[12582912]{0:T(1024)(128)(4,1)} %bitcast.137), calls=%async_computation.3 | async-start | bytes 8388608 | tf_op jit(solution)/shard_map/while
  368.1 13.6 %slice-start.1 = ((s8[12582912]{0:T(1024)(128)(4,1)}), s8[4194304]{0:T(1024)(128)(4,1)S(1)}, s32[]{:S(2)}) async-start(s8[12582912]{0:T(1024)(128)(4,1)} %bitcast.137), calls=%async_computation.4 | async-start | bytes 8388608 | tf_op jit(solution)/shard_map/while
  368.1 13.6 %slice-start.2 = ((s8[12582912]{0:T(1024)(128)(4,1)}), s8[4194304]{0:T(1024)(128)(4,1)S(1)}, s32[]{:S(2)}) async-start(s8[12582912]{0:T(1024)(128)(4,1)} %bitcast.137), calls=%async_computation.5 | async-start | bytes 8388608 | tf_op jit(solution)/shard_map/while
  368.1 13.6 %copy-start.5 = (pred[512,512]{0,1:T(8,128)(4,1)S(1)}, pred[512,512]{0,1:T(8,128)(4,1)}, u32[]{:S(2)}) copy-start(pred[512,512]{0,1:T(8,128)(4,1)} %broadcast_compare_fusion.5) | copy-start | bytes 786436 | tf_op jit(solution)/shard_map/while
  368.1 13.6 %copy-start.13 = (f32[12,512]{1,0:T(8,128)S(1)}, f32[12,512]{1,0:T(8,128)}, u32[]{:S(2)}) copy-start(f32[12,512]{1,0:T(8,128)} %dynamic-slice_bitcast_fusion.2) | copy-start | bytes 73732 | tf_op jit(solution)/shard_map/while
  381.7 7.2 copy-start.2
  398.9 6.4 copy-start.1
  398.9 7.3 copy-start.17
  398.9 7.9 copy-start.12
  410.0 13.6 %slice-start = ((s8[12582912]{0:T(1024)(128)(4,1)}), s8[4194304]{0:T(1024)(128)(4,1)S(1)}, s32[]{:S(2)}) async-start(s8[12582912]{0:T(1024)(128)(4,1)} %bitcast.137), calls=%async_computation.3 | async-start | bytes 8388608 | tf_op jit(solution)/shard_map/while
  410.0 13.6 %slice-start.1 = ((s8[12582912]{0:T(1024)(128)(4,1)}), s8[4194304]{0:T(1024)(128)(4,1)S(1)}, s32[]{:S(2)}) async-start(s8[12582912]{0:T(1024)(128)(4,1)} %bitcast.137), calls=%async_computation.4 | async-start | bytes 8388608 | tf_op jit(solution)/shard_map/while
  410.0 13.6 %slice-start.2 = ((s8[12582912]{0:T(1024)(128)(4,1)}), s8[4194304]{0:T(1024)(128)(4,1)S(1)}, s32[]{:S(2)}) async-start(s8[12582912]{0:T(1024)(128)(4,1)} %bitcast.137), calls=%async_computation.5 | async-start | bytes 8388608 | tf_op jit(solution)/shard_map/while
  410.0 13.6 %copy-start.5 = (pred[512,512]{0,1:T(8,128)(4,1)S(1)}, pred[512,512]{0,1:T(8,128)(4,1)}, u32[]{:S(2)}) copy-start(pred[512,512]{0,1:T(8,128)(4,1)} %broadcast_compare_fusion.5) | copy-start | bytes 786436 | tf_op jit(solution)/shard_map/while
  410.0 13.6 %copy-start.13 = (f32[12,512]{1,0:T(8,128)S(1)}, f32[12,512]{1,0:T(8,128)}, u32[]{:S(2)}) copy-start(f32[12,512]{1,0:T(8,128)} %dynamic-slice_bitcast_fusion.2) | copy-start | bytes 73732 | tf_op jit(solution)/shard_map/while
  423.7 7.2 copy-start.2
  (23 other events, 58.0 us)
Sparse Core Ops, SparseCore 0:
  179.2 93.1 reduce-scatter.1
  474.9 432.2 all-reduce.7
where the time goes:
time: 927 us; the launch traced here: 922 us
  waiting for transfers between devices  463 us (50%)
  matrix products  209 us (23%)
  local copies, waits for them, and re-layouts  99.4 us (11%)
  blocking collectives  92.1 us (10%)
  other arithmetic  41.7 us (4%)
  between operations  16.5 us (2%)
    unnamed x3, waiting for transfers between devices  370 us
    reduce_scatter x1, waiting for transfers between devices, per_device(): lax.psum_scatter(trans_dot(weights_low, embed_low) * inv_temp, 'batch', s...  93.2 us
    dot_general x5, matrix products, flat_dot(): return jnp.dot(left, right, preferred_element_type=jnp.float32)  66 us
    all_gather x1, blocking collectives, per_device(): lax.all_gather(embed_low, 'batch', axis=0, tiled=True)  48.1 us
    psum x1, blocking collectives, per_device(): loss_value = lax.psum(jnp.sum(log_norm - positive), 'batch') / total_seg  43.9 us
    dot_general x5, matrix products, back_dot(): lax.dot_general(left, right, (((1,), (1,)), ((), ())), preferred_element_...  35.5 us
    dot_general x5, matrix products, trans_dot(): lax.dot_general(left, right, (((0,), (0,)), ((), ())), preferred_element_...  32.8 us
    dot_general x2, matrix products, attend_back(): jnp.einsum('qhd,khd->hqk', grad_ctx, values, preferred_element_type=jnp.f...  27.2 us
  transfers between devices with their start and end apart: 2, of which 2 were waited for; matrix products, arithmetic and copies ran while one was open for 2% of the time, Pallas kernels for 0%

commit v1 on v0

v1 whole, which is shorter than its diff:
```python
import functools
import jax
import jax.numpy as jnp
from jax import lax
from jax.experimental import pallas as pl
from jax.experimental.pallas import tpu as pltpu

F32 = jnp.float32
BF16 = jnp.bfloat16
HEADS = 12
HEAD_DIM = 64
SEGS = 8
PAIR = 2 * HEAD_DIM
LN_EPS = 1e-12
NORM_EPS = 1e-06
MIB = 2**20


def dot_nn(a, b):
    return lax.dot_general(a, b, (((1,), (0,)), ((), ())), preferred_element_type=F32)


def dot_nt(a, b):
    return lax.dot_general(a, b, (((1,), (1,)), ((), ())), preferred_element_type=F32)


def dot_tn(a, b):
    return lax.dot_general(a, b, (((0,), (0,)), ((), ())), preferred_element_type=F32)


def gelu_parts(pre):
    half = 0.5 * pre
    cdf = 0.5 + 0.5 * lax.erf(pre * 0.7071067811865476)
    pdf = jnp.exp(-half * pre) * 0.3989422804014327
    return pre * cdf, cdf + pre * pdf


def normalize(resid):
    width = resid.shape[-1]
    average = jnp.sum(resid, axis=-1, keepdims=True) * (1.0 / width)
    centred = resid - average
    variance = jnp.sum(centred * centred, axis=-1, keepdims=True) * (1.0 / width)
    inv_std = lax.rsqrt(variance + LN_EPS)
    return centred * inv_std, inv_std


def forward_kernel(
    ids_ref, qb_ref, vb_ref, pb_ref, ag_ref, as_ref, ub_ref, db_ref, fg_ref, fs_ref,
    tok_hbm, wqkv_hbm, wp_hbm, wu_hbm, wd_hbm,
    exp_hbm, qkv_hbm, ctx_hbm, rinv_hbm, n1_hbm, low_hbm, act_hbm, der_hbm, n2_hbm, out_hbm,
    inv1_ref, inv2_ref, emb_ref, z_ref, invn_ref, cnt_ref,
    tok_s, wqkv_s, wp_s, wu_s, wd_s, qkv_s, ctx_s, rinv_s, bias_s, exp_s,
    n1_s, low_s, act_s, der_s, n2_s, out_s, in_sem, out_sem, exp_sem,
):
    rows, row_len = ids_ref.shape
    toks, width = tok_s.shape
    pairs = width // PAIR
    ff = wu_s.shape[1]

    loads = [
        pltpu.make_async_copy(src, dst, in_sem.at[i])
        for i, (src, dst) in enumerate(
            [(tok_hbm, tok_s), (wqkv_hbm, wqkv_s), (wp_hbm, wp_s), (wu_hbm, wu_s), (wd_hbm, wd_s)]
        )
    ]
    for cp in loads:
        cp.start()
    loads[0].wait()
    loads[1].wait()

    tok = tok_s[...]
    blk = 256
    for j in range(3 * width // blk):
        piece = dot_nn(tok, wqkv_s[:, j * blk : (j + 1) * blk])
        third, off = divmod(j * blk, width)
        if third == 0:
            piece = piece + qb_ref[:, off : off + blk]
        elif third == 2:
            piece = piece + vb_ref[:, off : off + blk]
        qkv_s[:, j * blk : (j + 1) * blk] = piece.astype(BF16)
    qkv_out = pltpu.make_async_copy(qkv_s, qkv_hbm, out_sem.at[0])
    qkv_out.start()

    lane = lax.broadcasted_iota(jnp.int32, (row_len, PAIR), 1)
    first = lane < HEAD_DIM
    ones = jnp.ones((row_len, PAIR), BF16)

    for r in range(rows):
        ids_row = ids_ref[r : r + 1, :].astype(F32)
        ids_col = jnp.transpose(jnp.broadcast_to(ids_row, (128, row_len)))
        for c in range(row_len // 128):
            bias_s[r, :, c * 128 : (c + 1) * 128] = jnp.where(
                ids_col == ids_row[:, c * 128 : (c + 1) * 128], 0.0, -1e9
            )

    def attend(it, carry):
        r = it // pairs
        p = it % pairs
        rsl = pl.ds(pl.multiple_of(r * row_len, row_len), row_len)
        col = lambda third: pl.ds(pl.multiple_of(third * width + p * PAIR, PAIR), PAIR)
        q = qkv_s[rsl, col(0)] * jnp.asarray(HEAD_DIM**-0.5, BF16)
        k = qkv_s[rsl, col(1)]
        v = jnp.concatenate([qkv_s[rsl, col(2)], ones], axis=1)
        slot = lax.rem(it, 2)

        @pl.when(it >= 2)
        def _():
            pltpu.make_async_copy(exp_s.at[slot], exp_hbm.at[it], exp_sem.at[slot]).wait()

        parts = []
        for h in range(2):
            qh = jnp.where(first if h == 0 else ~first, q, jnp.zeros_like(q))
            s = dot_nt(qh, k) + bias_s[r]
            e = jnp.exp(s - jnp.max(s, axis=1, keepdims=True)).astype(BF16)
            exp_s[slot, h] = e
            oe = dot_nn(e, v)
            rinv = 1.0 / oe[:, PAIR:]
            parts.append((oe[:, :PAIR] * rinv, rinv))
        ctx_s[rsl, pl.ds(pl.multiple_of(p * PAIR, PAIR), PAIR)] = jnp.where(
            first, parts[0][0], parts[1][0]
        ).astype(BF16)
        rinv_s[rsl, pl.ds(pl.multiple_of(p * PAIR, PAIR), PAIR)] = jnp.where(
            first, parts[0][1], parts[1][1]
        )
        pltpu.make_async_copy(exp_s.at[slot], exp_hbm.at[it], exp_sem.at[slot]).start()
        return carry

    lax.fori_loop(0, rows * pairs, attend, 0)
    ctx_out = pltpu.make_async_copy(ctx_s, ctx_hbm, out_sem.at[1])
    ctx_out.start()
    rinv_out = pltpu.make_async_copy(rinv_s, rinv_hbm, out_sem.at[2])
    rinv_out.start()
    for cp in loads[2:]:
        cp.wait()

    outs = [(n1_s, n1_hbm), (low_s, low_hbm), (act_s, act_hbm), (der_s, der_hbm), (n2_s, n2_hbm), (out_s, out_hbm)]

    def ffn(r, carry):
        rsl = pl.ds(pl.multiple_of(r * row_len, row_len), row_len)
        resid = tok_s[rsl, :].astype(F32) + (dot_nn(ctx_s[rsl, :], wp_s[...]) + pb_ref[...])
        normed, inv_std = normalize(resid)
        n1_s[rsl, :] = normed
        inv1_ref[rsl, :] = jnp.broadcast_to(inv_std, (row_len, 128))
        first_norm = normed * ag_ref[...] + as_ref[...]
        low = first_norm.astype(BF16)
        low_s[rsl, :] = low
        for j in range(ff // blk):
            pre = dot_nn(low, wu_s[:, j * blk : (j + 1) * blk]) + ub_ref[:, j * blk : (j + 1) * blk]
            act, der = gelu_parts(pre)
            act_s[rsl, j * blk : (j + 1) * blk] = act.astype(BF16)
            der_s[rsl, j * blk : (j + 1) * blk] = der.astype(BF16)
        down = dot_nn(act_s[rsl, :], wd_s[...]) + db_ref[...]
        normed2, inv_std2 = normalize(first_norm + down)
        n2_s[rsl, :] = normed2
        inv2_ref[rsl, :] = jnp.broadcast_to(inv_std2, (row_len, 128))
        y = normed2 * fg_ref[...] + fs_ref[...]
        high = y.astype(BF16)
        out_s[rsl, :] = high
        rest = (y - high.astype(F32)).astype(BF16)
        seg = lax.broadcasted_iota(jnp.int32, (SEGS, row_len), 0)
        member = (seg == ids_ref[pl.ds(r, 1), :]).astype(F32)
        count = jnp.sum(member, axis=1, keepdims=True)
        member = member.astype(BF16)
        pooled = (dot_nn(member, high) + dot_nn(member, rest)) / count
        inv_norm = lax.rsqrt(jnp.sum(pooled * pooled, axis=1, keepdims=True) + NORM_EPS)
        z = pooled * inv_norm
        ssl = pl.ds(pl.multiple_of(r * SEGS, SEGS), SEGS)
        z_ref[ssl, :] = z
        invn_ref[ssl, :] = jnp.broadcast_to(inv_norm, (SEGS, 128))
        cnt_ref[ssl, :] = jnp.broadcast_to(count, (SEGS, 128))
        for i, (src, dst) in enumerate(outs):
            pltpu.make_async_copy(src.at[rsl, :], dst.at[rsl, :], out_sem.at[3 + i]).start()
        return carry

    lax.fori_loop(0, rows, ffn, 0)
    emb_ref[...] = z_ref[...].astype(BF16)
    for i, (src, dst) in enumerate(outs):
        pltpu.make_async_copy(src, dst, out_sem.at[3 + i]).wait()
    qkv_out.wait()
    ctx_out.wait()
    rinv_out.wait()
    for slot in range(2):
        pltpu.make_async_copy(exp_s.at[slot], exp_hbm.at[0], exp_sem.at[slot]).wait()


def forward_call(tokens, ids, wqkv, qb, vb, wp, pb, ag, ash, wu, ub, wd, db, fg, fs):
    toks, width = tokens.shape
    rows, row_len = ids.shape
    ff = wu.shape[1]
    pairs = width // PAIR
    segs = rows * SEGS
    sds = jax.ShapeDtypeStruct
    row = lambda v: v.reshape(1, -1)
    vm = pl.BlockSpec(memory_space=pltpu.VMEM)
    hb = pl.BlockSpec(memory_space=pl.ANY)
    return pl.pallas_call(
        forward_kernel,
        out_shape=(
            sds((rows * pairs, 2, row_len, row_len), BF16),
            sds((toks, 3 * width), BF16),
            sds((toks, width), BF16),
            sds((toks, width), F32),
            sds((toks, width), F32),
            sds((toks, width), BF16),
            sds((toks, ff), BF16),
            sds((toks, ff), BF16),
            sds((toks, width), F32),
            sds((toks, width), BF16),
            sds((toks, 128), F32),
            sds((toks, 128), F32),
            sds((segs, width), BF16),
            sds((segs, width), F32),
            sds((segs, 128), F32),
            sds((segs, 128), F32),
        ),
        in_specs=[vm] * 10 + [hb] * 5,
        out_specs=[hb] * 10 + [vm] * 6,
        scratch_shapes=[
            pltpu.VMEM((toks, width), BF16),
            pltpu.VMEM(wqkv.shape, BF16),
            pltpu.VMEM(wp.shape, BF16),
            pltpu.VMEM(wu.shape, BF16),
            pltpu.VMEM(wd.shape, BF16),
            pltpu.VMEM((toks, 3 * width), BF16),
            pltpu.VMEM((toks, width), BF16),
            pltpu.VMEM((toks, width), F32),
            pltpu.VMEM((rows, row_len, row_len), F32),
            pltpu.VMEM((2, 2, row_len, row_len), BF16),
            pltpu.VMEM((toks, width), F32),
            pltpu.VMEM((toks, width), BF16),
            pltpu.VMEM((toks, ff), BF16),
            pltpu.VMEM((toks, ff), BF16),
            pltpu.VMEM((toks, width), F32),
            pltpu.VMEM((toks, width), BF16),
            pltpu.SemaphoreType.DMA((5,)),
            pltpu.SemaphoreType.DMA((9,)),
            pltpu.SemaphoreType.DMA((2,)),
        ],
        compiler_params=pltpu.CompilerParams(vmem_limit_bytes=60 * MIB),
        name="forward",
    )(ids, row(qb), row(vb), row(pb), row(ag), row(ash), row(ub), row(db), row(fg), row(fs), tokens, wqkv, wp, wu, wd)


MESH = pl.DeviceIdType.MESH
INV_TEMP = 100.0
NEG = -1000000000.0


def axis_groups(n):
    groups = []
    rest = n // 2
    while rest > 1:
        size = 4 if rest % 4 == 0 else (2 if rest % 2 == 0 else rest)
        groups.append(size)
        rest //= size
    return groups + [2]


def digits_of(me, groups):
    digits = []
    for size in reversed(groups):
        digits.append(lax.rem(me, size))
        me = me // size
    return digits[::-1]


def index_of(digits, groups):
    me = 0
    for digit, size in zip(digits, groups):
        me = me * size + digit
    return me


def contrast_kernel(groups, msg_ref, z_ref, invn_ref, cnt_ref, loss_ref, gp_ref, all_s, send_sem, recv_sem):
    n = 1
    for size in groups:
        n *= size
    me = lax.axis_index("batch")
    mine = digits_of(me, groups)
    seg_here, wide = msg_ref.shape
    width = z_ref.shape[1]
    total = n * seg_here
    stages = len(groups)

    def peer(stage, step):
        other = lax.rem(mine[stage] + step, groups[stage])
        return other, index_of(mine[:stage] + [other] + mine[stage + 1 :], groups)

    barrier = pltpu.get_barrier_semaphore()
    hops = 0
    for stage in range(stages):
        for step in range(1, groups[stage]):
            pl.semaphore_signal(barrier, inc=1, device_id=(peer(stage, step)[1],), device_id_type=MESH)
            hops += 1
    all_s[tuple(mine)] = msg_ref[...]
    pl.semaphore_wait(barrier, hops)

    slot = 0
    for stage in range(stages):
        copies = []
        for step in range(1, groups[stage]):
            block = all_s.at[(slice(None),) * stage + tuple(mine[stage:])]
            copies.append(
                pltpu.make_async_remote_copy(
                    src_ref=block,
                    dst_ref=block,
                    send_sem=send_sem.at[slot],
                    recv_sem=recv_sem.at[slot],
                    device_id=(peer(stage, step)[1],),
                    device_id_type=MESH,
                )
            )
            slot += 1
        for cp in copies:
            cp.start()
        for cp in copies:
            cp.wait()

    every = all_s[...].reshape(total, wide)
    emb = every[:, :width]
    own = msg_ref[:, :width]
    z = z_ref[...]
    own_row = (me * seg_here).astype(F32)
    own_pair = msg_ref[:, width : width + 128].astype(F32)
    own_pair = own_pair[:, 0:1] * 256.0 + own_pair[:, 1:2]

    scores = dot_nt(own, emb) * INV_TEMP
    column = lax.broadcasted_iota(jnp.int32, scores.shape, 1).astype(F32)
    row = lax.broadcasted_iota(jnp.int32, scores.shape, 0).astype(F32) + own_row
    masked = jnp.where(column == row, NEG, scores)
    peak = jnp.max(masked, axis=1, keepdims=True)
    log_norm = peak + jnp.log(jnp.sum(jnp.exp(masked - peak), axis=1, keepdims=True))
    weight = jnp.exp(masked - log_norm) - (column == own_pair).astype(F32)
    grad = dot_nn(weight.astype(BF16), emb)

    blk = min(total, 512)
    loss = jnp.zeros((1, 1), F32)
    for b in range(total // blk):
        part = emb[b * blk : (b + 1) * blk]
        pair = every[b * blk : (b + 1) * blk, width:].astype(F32)
        pair = pair[:, 0:1] * 256.0 + pair[:, 1:2]
        scores = dot_nt(part, emb) * INV_TEMP
        column = lax.broadcasted_iota(jnp.int32, scores.shape, 1).astype(F32)
        row = lax.broadcasted_iota(jnp.int32, scores.shape, 0).astype(F32) + float(b * blk)
        masked = jnp.where(column == row, NEG, scores)
        peak = jnp.max(masked, axis=1, keepdims=True)
        log_norm = peak + jnp.log(jnp.sum(jnp.exp(masked - peak), axis=1, keepdims=True))
        positive = jnp.sum(jnp.where(column == pair, scores, 0.0), axis=1, keepdims=True)
        loss = loss + jnp.sum(log_norm - positive, axis=0, keepdims=True)
        scores = dot_nt(part, own) * INV_TEMP
        column = lax.broadcasted_iota(jnp.int32, scores.shape, 1).astype(F32) + own_row
        row = lax.broadcasted_iota(jnp.int32, scores.shape, 0).astype(F32) + float(b * blk)
        weight = jnp.where(column == row, 0.0, jnp.exp(jnp.where(column == row, NEG, scores) - log_norm))
        weight = weight - (column == pair).astype(F32)
        grad = grad + dot_tn(weight.astype(BF16), part)
    loss_ref[...] = jnp.broadcast_to(loss * (1.0 / total), loss_ref.shape)
    grad = grad * INV_TEMP
    pooled_grad = invn_ref[:, 0:1] * (grad - z * jnp.sum(grad * z, axis=1, keepdims=True))
    gp_ref[...] = pooled_grad / cnt_ref[:, 0:1]


def contrast_call(n, emb_low, z, invn, cnt, pair_index):
    groups = axis_groups(n)
    seg_here, width = emb_low.shape
    high = (pair_index // 256).astype(BF16)[:, None]
    rest = (pair_index % 256).astype(BF16)[:, None]
    msg = jnp.concatenate([emb_low, high, rest, jnp.zeros((seg_here, 126), BF16)], axis=1)
    copies = sum(size - 1 for size in groups)
    vm = pl.BlockSpec(memory_space=pltpu.VMEM)
    return pl.pallas_call(
        functools.partial(contrast_kernel, groups),
        out_shape=(jax.ShapeDtypeStruct((8, 128), F32), jax.ShapeDtypeStruct((seg_here, width), F32)),
        in_specs=[vm] * 4,
        out_specs=[vm] * 2,
        scratch_shapes=[
            pltpu.VMEM(tuple(groups) + msg.shape, BF16),
            pltpu.SemaphoreType.DMA((copies,)),
            pltpu.SemaphoreType.DMA((copies,)),
        ],
        compiler_params=pltpu.CompilerParams(collective_id=0, has_side_effects=True, vmem_limit_bytes=56 * MIB),
        name="contrast",
    )(msg, z, invn, cnt)

from jax.sharding import PartitionSpec as P


def norm_back(grad_out, normed, inv_std, gain):
    grad_n = grad_out * gain
    return inv_std * (
        grad_n
        - jnp.mean(grad_n, axis=-1, keepdims=True)
        - normed * jnp.mean(grad_n * normed, axis=-1, keepdims=True)
    )


def attend_back(entry):
    qkv_row, exps, rinv, ctx, grad_row = entry
    row_len = qkv_row.shape[0]
    split = qkv_row.reshape(row_len, 3, HEADS, HEAD_DIM)
    queries, key_vecs, values = split[:, 0], split[:, 1], split[:, 2]
    exps = exps.reshape(HEADS, row_len, row_len)
    scaled = (grad_row.astype(F32) * rinv).astype(BF16)
    delta = jnp.sum(scaled.astype(F32).reshape(row_len, HEADS, HEAD_DIM) * ctx.astype(F32).reshape(row_len, HEADS, HEAD_DIM), axis=-1)
    scaled = scaled.reshape(row_len, HEADS, HEAD_DIM)
    grad_probs = jnp.einsum("qhd,khd->hqk", scaled, values, preferred_element_type=F32)
    grad_values = jnp.einsum("hqk,qhd->khd", exps, scaled, preferred_element_type=F32)
    grad_scores = (exps.astype(F32) * (grad_probs - delta.T[..., None])).astype(BF16)
    grad_queries = jnp.einsum("hqk,khd->qhd", grad_scores, key_vecs, preferred_element_type=F32) * HEAD_DIM**-0.5
    grad_keys = jnp.einsum("hqk,qhd->khd", grad_scores, queries, preferred_element_type=F32) * HEAD_DIM**-0.5
    stacked = jnp.stack([grad_queries, grad_keys, grad_values], axis=1)
    return stacked.reshape(row_len, 3 * HEADS * HEAD_DIM).astype(BF16)


def per_device(
    tokens, segment_ids, pair_index, qkv_weight, query_bias, value_bias, proj_weight, proj_bias,
    attn_gain, attn_shift, up_weight, up_bias, down_weight, down_bias, ffn_gain, ffn_shift,
):
    n = lax.axis_size("batch")
    rows, row_len = segment_ids.shape
    toks, width = tokens.shape
    (exps, qkv, context, rinv, normed_one, first_low, acted, deriv, normed_two, layer_out,
     inv_one, inv_two, emb_low, z, invn, cnt) = forward_call(
        tokens, segment_ids, qkv_weight, query_bias, value_bias, proj_weight, proj_bias, attn_gain, attn_shift,
        up_weight, up_bias, down_weight, down_bias, ffn_gain, ffn_shift)
    loss, grad_seg = contrast_call(n, emb_low, z, invn, cnt, pair_index)
    inv_one = inv_one[:, :1]
    inv_two = inv_two[:, :1]
    row_base = (jnp.arange(rows, dtype=jnp.int32) * SEGS)[:, None]
    local_ids = jnp.where(segment_ids >= 0, segment_ids + row_base, -1).reshape(toks)
    member = (local_ids[None, :] == jnp.arange(rows * SEGS, dtype=jnp.int32)[:, None]).astype(F32)
    grad_y = lax.dot_general(member, grad_seg, (((0,), (0,)), ((), ())), precision=lax.Precision.HIGHEST)
    ffn_gain_part = jnp.sum(grad_y * normed_two, axis=0)
    ffn_shift_part = jnp.sum(grad_y, axis=0)
    grad_r2 = norm_back(grad_y, normed_two, inv_two, ffn_gain)
    grad_down_low = grad_r2.astype(BF16)
    down_bias_part = jnp.sum(grad_down_low.astype(F32), axis=0)
    down_weight_part = dot_tn(acted, grad_down_low)
    grad_up_low = (dot_nt(grad_down_low, down_weight) * deriv.astype(F32)).astype(BF16)
    up_bias_part = jnp.sum(grad_up_low.astype(F32), axis=0)
    up_weight_part = dot_tn(first_low, grad_up_low)
    grad_first = grad_r2 + dot_nt(grad_up_low, up_weight)
    attn_gain_part = jnp.sum(grad_first * normed_one, axis=0)
    attn_shift_part = jnp.sum(grad_first, axis=0)
    grad_r1 = norm_back(grad_first, normed_one, inv_one, attn_gain)
    grad_att_low = grad_r1.astype(BF16)
    proj_bias_part = jnp.sum(grad_att_low.astype(F32), axis=0)
    proj_weight_part = dot_tn(context, grad_att_low)
    grad_context = dot_nt(grad_att_low, proj_weight).astype(BF16)
    by_row = lambda v: v.reshape(rows, row_len, -1)
    grad_qkv = lax.map(
        attend_back,
        (by_row(qkv), exps.reshape(rows, -1, 2, row_len, row_len), by_row(rinv), by_row(context), by_row(grad_context)),
    ).reshape(toks, 3 * width)
    qkv_bias_part = jnp.sum(grad_qkv.astype(F32), axis=0)
    qkv_weight_part = dot_tn(tokens, grad_qkv)
    tokens_grad = grad_r1 + dot_nt(grad_qkv, qkv_weight)
    scatter = lambda v: lax.psum_scatter(v.reshape(-1), "batch", scatter_dimension=0, tiled=True)
    sums = lax.psum(
        (qkv_bias_part[:width], qkv_bias_part[2 * width :], proj_bias_part, attn_gain_part, attn_shift_part,
         up_bias_part, down_bias_part, ffn_gain_part, ffn_shift_part),
        "batch",
    )
    return (loss[0, 0], layer_out, tokens_grad, scatter(qkv_weight_part), scatter(proj_weight_part),
            scatter(up_weight_part), scatter(down_weight_part)) + tuple(sums)


def solution(mesh):
    split, whole = P("batch"), P()
    return jax.shard_map(
        per_device,
        mesh=mesh,
        in_specs=(P("batch", None), P("batch", None), split) + (whole,) * 13,
        out_specs=(whole, P("batch", None), P("batch", None)) + (split,) * 4 + (whole,) * 9,
        check_vma=False,
    )
```

time: 927 us -> 710 us (0.77)
  matrix products: 209 us -> 83.7 us
  waiting for transfers between devices: 463 us -> 376 us
  Pallas kernels: 0 us -> 65.7 us
  blocking collectives: 92.1 us -> 43.2 us
  other arithmetic: 41.7 us -> 13.1 us
    dot_general x29 -> x15, matrix products: 206 us -> 79.7 us  [the longest x4 31.8 us: dot_nt(): lax.dot_general(a, b, (((1,), (1,)), ((), ())), preferred_element_type=F32)]
    reduce_scatter x1 -> x0, waiting for transfers between devices: 93.2 us -> none  [per_device(): lax.psum_scatter(trans_dot(weights_low, embed_low) * inv_temp, 'batch', s...]
    pallas_call x0 -> x2, Pallas kernels: none -> 65.7 us  [the longest x1 46.5 us: forward_call(): pl.pallas_call(forward_kernel, out_shape=(sds((rows * pairs, 2, row_len,...]
    all_gather x1 -> x0, blocking collectives: 48.1 us -> none  [per_device(): lax.all_gather(embed_low, 'batch', axis=0, tiled=True)]
    dynamic_slice x12 -> x16, local copies, waits for them, and re-layouts: 13.9 us -> 34.4 us  [per_device(): lax.map(attend_back, (by_row(qkv), exps.reshape(rows, -1, 2, row_len, row...]
    convert_element_type x3 -> x2, other arithmetic: 14.3 us -> 0.51 us  [attend_back(): scaled = (grad_row.astype(F32) * rinv).astype(BF16)]
    reduce_sum x11 -> x5, other arithmetic: 21.9 us -> 9.21 us  [the longest x1 4.01 us: per_device(): proj_bias_part = jnp.sum(grad_att_low.astype(F32), axis=0)]
    unnamed x99 -> x52, local copies, waits for them, and re-layouts: 24.4 us -> 12.8 us
  transfers between devices with their start and end apart: 2 -> 1, of which waited for: 2 -> 1; matrix products, arithmetic and copies ran while one was open for 2% -> 2% of each run, Pallas kernels for 0% -> 0%
where the time goes in v1:
time: 710 us; the launch traced here: 700 us
  waiting for transfers between devices  376 us (53%)
  local copies, waits for them, and re-layouts  103 us (15%)
  matrix products  83.7 us (12%)
  Pallas kernels  65.7 us (9%)
  blocking collectives  43.2 us (6%)
  between operations  14.7 us (2%)
  other arithmetic  13.1 us (2%)
    unnamed x2, waiting for transfers between devices  376 us
    pallas_call x1, Pallas kernels, forward_call(): pl.pallas_call(forward_kernel, out_shape=(sds((rows * pairs, 2, row_len,...  46.5 us
    psum x1, blocking collectives, per_device(): lax.psum((qkv_bias_part[:width], qkv_bias_part[2 * width:], proj_bias_par...  43.2 us
    dynamic_slice x16, local copies, waits for them, and re-layouts, per_device(): lax.map(attend_back, (by_row(qkv), exps.reshape(rows, -1, 2, row_len, row...  34.4 us
    dot_general x4, matrix products, dot_nt(): lax.dot_general(a, b, (((1,), (1,)), ((), ())), preferred_element_type=F32)  31.8 us
    dot_general x4, matrix products, dot_tn(): lax.dot_general(a, b, (((0,), (0,)), ((), ())), preferred_element_type=F32)  26.9 us
    reshape x3, local copies, waits for them, and re-layouts, per_device(): v.reshape(-1)  20.4 us
    pallas_call x1, Pallas kernels, contrast_call(): pl.pallas_call(functools.partial(contrast_kernel, groups), out_shape=(jax...  19.3 us
  transfers between devices with their start and end apart: 1, of which 1 were waited for; matrix products, arithmetic and copies ran while one was open for 2% of the time, Pallas kernels for 0%

profile of v1, /device:TPU:0, one launch (start us, length us, event | category | flops | bytes accessed | tf_op | source)
XLA Modules:
  0.0 700.1 jit_solution(16688006733395448766)
XLA Ops:
  19.1 46.5 %forward.1 = (bf16[12,2,512,512]{3,2,1,0:T(8,128)(2,1)}, bf16[1024,2304]{1,0:T(8,128)(2,1)}, bf16[1024,768]{1,0:T(8,128)(2,1)S(1)}, f32[1024,768]{1,0:T(8,128)},...) custom-call(s32[2,512]{1,0:T(2,128)} %ids_ref.1, ...), custom_call_target="tpu_custom_call" | custom-call | tf_op jit(solution)/shard_map/forward/pallas_call | solution.py:196
  65.6 1.4 maximum_maximum_fusion.msg_ref
  67.0 19.3 %contrast.1 = (f32[8,128]{1,0:T(8,128)}, f32[16,768]{1,0:T(8,128)}) custom-call(bf16[16,896]{1,0:T(8,128)(2,1)} %maximum_maximum_fusion.msg_ref, f32[16,768]{1,0:T(8,128)} %get-tuple-element.72.z_ref, f32[16,128]{1,0:T(8,128)} %get-tuple-element.73.invn_ref, f32[16,128]{1,0:T(8,128)} %get-tuple-element.74.cnt_ref), custom_call_target="tpu_custom_call" | custom-call | tf_op jit(solution)/shard_map/contrast/pallas_call | solution.py:370
  86.3 4.9 multiply_reduce_fusion
  91.6 1.7 convert_reduce_fusion.2
  93.6 10.9 %convert_reduce_fusion = (f32[3072]{0:T(1024)}, bf16[1024,3072]{1,0:T(8,128)(2,1)}) fusion(bf16[1024,3072]{1,0:T(8,128)(2,1)} %get-tuple-element.81, bf16[3072,768]{1,0:T(8,128)(2,1)S(1)} %bitcast.119, f32[1024,768]{1,0:T(8,128)S(1)} %get-tuple-element.147), kind=kOutput, calls=%fused_computation.20 | convolution fusion | flops 4848350208 | bytes 20459520 | tf_op jit(solution)/shard_map/dot_general | solution.py:24
  104.6 9.7 %multiply_reduce_fusion.1 = (f32[768]{0:T(1024)}, f32[1024]{0:T(1024)S(1)}, f32[1024]{0:T(1024)S(1)}, f32[768]{0:T(1024)}, f32[1024,768]{1,0:T(8,128)}) fusion(f32[1024,768]{1,0:T(8,128)S(1)} %copy-done.11, f32[768]{0:T(1024)S(1)} %copy-done.18, f32[1024,768]{1,0:T(8,128)S(1)} %get-tuple-element.147, bf16[1024,3072]{1,0:T(8,128)(2,1)} %get-tuple-element.159, ...), kind=kOutput, calls=%fused_computation.27 | convolution fusion | flops 4838125568 | bytes 20464640 | tf_op jit(solution)/shard_map/dot_general | solution.py:24
  114.3 4.0 convert_reduce_fusion.3
  118.3 2.6 convolution_convert_fusion.1
  120.9 2.9 fusion.9
  123.8 64.1 %while.10 = (s32[]{:T(128)}, bf16[2,512,2304]{1,2,0:T(8,128)(2,1)}, bf16[2,512,2304]{2,1,0:T(8,128)(2,1)}, bf16[2,6,2,512,512]{4,3,2,1,0:T(8,128)(2,1)}, bf16[2,...) while((s32[]{:T(128)}, bf16[2,512,2304]{1,2,0:T(8,128)(2,1)}, ...), condition=%wide.region_6.7_spmd, body=%wide.region_4.6_spmd.sunk | while | flops 1630267392 | bytes 163635536 | solution.py:450
  125.1 2.7 constant_dynamic-slice_fusion.9
  127.8 1.9 copy.64
  129.7 2.4 constant_dynamic-slice_fusion.10
  132.6 3.6 constant_dynamic-slice_fusion.11
  136.2 2.6 fusion.48
  139.6 3.3 constant_dynamic-slice_fusion.12
  142.9 2.8 copy.67
  145.7 4.4 multiply_convert_fusion.8
  151.2 2.0 fusion.51
  153.9 2.1 copy-done.3
  157.1 2.7 constant_dynamic-slice_fusion.9
  159.8 1.9 copy.64
  161.7 2.4 constant_dynamic-slice_fusion.10
  164.6 3.6 constant_dynamic-slice_fusion.11
  168.2 2.6 fusion.48
  171.6 3.3 constant_dynamic-slice_fusion.12
  174.8 2.8 copy.67
  177.7 4.4 multiply_convert_fusion.8
  183.2 2.0 fusion.51
  185.8 2.1 copy-done.3
  187.9 6.8 copy.52
  194.8 8.1 %convolution_bitcast_fusion = f32[768,2304]{0,1:T(8,128)} fusion(bf16[1024,2304]{1,0:T(8,128)(2,1)} %bitcast.122, bf16[1024,768]{1,0:T(8,128)(2,1)S(1)} %copy-done.13), kind=kOutput, calls=%fused_computation.23 | convolution fusion | flops 3623878656 | bytes 13369344 | tf_op jit(solution)/shard_map/dot_general | solution.py:28
  202.9 8.0 %copy.53 = f32[768,2304]{1,0:T(8,128)} copy(f32[768,2304]{0,1:T(8,128)} %convolution_bitcast_fusion) | data formatting | bytes 14155776 | tf_op jit(solution)/shard_map/dot_general | solution.py:28
  210.9 8.1 %reshape.161 = f32[1769472]{0:T(1024)} reshape(f32[768,2304]{1,0:T(8,128)} %copy.53) | data formatting | bytes 14155776 | tf_op jit(solution)/shard_map/reshape | solution.py:457
  219.0 1.5 reshape.162
  220.5 8.1 %convolution_bitcast_fusion.1 = f32[96,24,8,128]{3,2,1,0:T(8,128)S(1)} fusion(bf16[1024,768]{1,0:T(8,128)(2,1)} %get-tuple-element.88, bf16[1024,3072]{1,0:T(8,128)(2,1)} %get-tuple-element.159), kind=kOutput, calls=%fused_computation.24 | convolution fusion | flops 4831838208 | bytes 17301504 | tf_op jit(solution)/shard_map/dot_general | solution.py:28
  228.7 5.9 copy.59
  234.6 7.8 %fusion.12 = f32[3072,768]{1,0:T(8,128)} fusion(bf16[1024,3072]{1,0:T(8,128)(2,1)S(1)} %bitcast.128, f32[1024,768]{1,0:T(8,128)S(1)} %copy-done.10), kind=kOutput, calls=%fused_computation.62 | convolution fusion | flops 4832624640 | bytes 18874368 | tf_op jit(solution)/shard_map/dot_general | solution.py:28
  242.3 10.8 %reshape.164 = f32[2359296]{0:T(1024)} reshape(f32[3072,768]{1,0:T(8,128)} %fusion.12) | data formatting | bytes 18874368 | tf_op jit(solution)/shard_map/reshape | solution.py:457
  254.6 3.0 convert_reduce_fusion.1
  258.2 43.2 %all-reduce.4 = (f32[768]{0:T(1024)}, f32[768]{0:T(1024)}, f32[768]{0:T(1024)}, f32[768]{0:T(1024)}, f32[768]{0:T(1024)}, /*index=5*/f32[3072]{0:T(1024)}, f32[768]{0:T(1024)}, f32[768]{0:T(1024)}, f32[768]{0:T(1024)}) all-reduce(f32[768]{0:T(1024)} %get-tuple-element.153, ...), channel_id=1, replica_groups=mesh['batch'=32] {'batch'}, use_global_device_ids=true, to_apply=%region_12.13 | all-reduce | flops 9216 | bytes 73728 | tf_op jit(solution)/shard_map/psum | solution.py:458
  301.4 8.5 %convolution_add_fusion.1 = f32[1024,768]{1,0:T(8,128)} fusion(f32[1024,768]{1,0:T(8,128)} %copy-done.8, bf16[1024,2304]{1,0:T(8,128)(2,1)} %bitcast.123, bf16[768,2304]{1,0:T(8,128)(2,1)S(1)} %copy-done.7), kind=kOutput, calls=%fused_computation.36 | convolution fusion | flops 3624665088 | bytes 14548992 | tf_op jit(solution)/shard_map/dot_general | solution.py:24
  309.9 376.4 %all-reduce.8.cloned.1.call-done = (f32[1769472]{0:T(1024)}, f32[589824]{0:T(1024)}, f32[2359296]{0:T(1024)}, f32[2359296]{0:T(1024)}) async-done(((f32[1769472]{0:T(1024)}, f32[589824]{0:T(1024)}, f32[2359296]{0:T(1024)}, f32[2359296]{0:T(1024)}), (f32[1769472]{0:T(1024)}, f32[589824]{0:T(1024)}, f32[2359296]{0:T(1024)}, f32[2359296]{0:T(1024)})) %all-reduce.8.cloned.1.call-update) | async-done | bytes 28311568
  686.3 1.7 dynamic-slice.2
  688.0 1.7 dynamic-slice.3
  689.7 1.6 dynamic-slice
  691.3 1.5 dynamic-slice.1
  (120 shorter events, 22.9 us)
Async XLA Ops:
  7.2 679.1 %all-reduce.8.cloned.1.call-start = ((), (), s32[]{:S(2)}) async-start(), calls=%async_computation | async-start | bytes 56623104
  19.1 67.2 %copy-start.17 = (f32[768]{0:T(1024)S(1)}, f32[768]{0:T(1024)}, u32[]{:S(2)}) copy-start(f32[768]{0:T(1024)} %param.32) | copy-start | bytes 9220
  86.3 5.0 copy-start.15
  86.3 4.9 copy-start.16
  86.3 5.3 copy-start.4
  91.2 2.2 slice-start.2
  91.6 2.0 slice-start.3
  91.6 13.0 %slice-start.4 = ((s8[4718592]{0:T(1024)(128)(4,1)}), s8[4194304]{0:T(1024)(128)(4,1)S(1)}, s32[]{:S(2)}) async-start(s8[4718592]{0:T(1024)(128)(4,1)} %bitcast.120), calls=%async_computation.5 | async-start | bytes 8388608
  93.3 11.3 %copy-start.9 = (f32[1024,768]{1,0:T(8,128)}, f32[1024,768]{1,0:T(8,128)S(1)}, u32[]{:S(2)}) copy-start(f32[1024,768]{1,0:T(8,128)S(1)} %get-tuple-element.147) | copy-start | bytes 9437188
  93.6 10.9 %slice-start.5 = ((s8[4718592]{0:T(1024)(128)(4,1)}), s8[524288]{0:T(1024)(128)(4,1)S(1)}, s32[]{:S(2)}) async-start(s8[4718592]{0:T(1024)(128)(4,1)} %bitcast.120), calls=%async_computation.6 | async-start | bytes 1048576
  93.6 10.9 %copy-start.11 = (f32[1024,768]{1,0:T(8,128)S(1)}, f32[1024,768]{1,0:T(8,128)}, u32[]{:S(2)}) copy-start(f32[1024,768]{1,0:T(8,128)} %get-tuple-element.82) | copy-start | bytes 9437188
  93.6 10.9 %copy-start.18 = (f32[768]{0:T(1024)S(1)}, f32[768]{0:T(1024)}, u32[]{:S(2)}) copy-start(f32[768]{0:T(1024)} %param.26) | copy-start | bytes 9220
  114.3 4.0 copy-start.14
  118.3 2.6 copy-start.8
  124.0 1.1 copy-start.5
  136.2 2.8 copy-start
  136.2 2.8 copy-start.1
  145.7 7.8 %slice-start = ((s8[4718592]{0:T(1024)(128)(4,1)}), s8[4194304]{0:T(1024)(128)(4,1)S(1)}, s32[]{:S(2)}) async-start(s8[4718592]{0:T(1024)(128)(4,1)} %bitcast.114), calls=%async_computation.1 | async-start | bytes 8388608 | tf_op jit(solution)/shard_map/while
  150.1 3.5 slice-start.1
  151.2 2.0 copy-start.2
  153.5 2.4 copy-start.6
  153.9 2.1 copy-start.3
  156.0 1.1 copy-start.5
  168.2 2.8 copy-start
  168.2 2.8 copy-start.1
  177.7 7.8 %slice-start = ((s8[4718592]{0:T(1024)(128)(4,1)}), s8[4194304]{0:T(1024)(128)(4,1)S(1)}, s32[]{:S(2)}) async-start(s8[4718592]{0:T(1024)(128)(4,1)} %bitcast.114), calls=%async_computation.1 | async-start | bytes 8388608 | tf_op jit(solution)/shard_map/while
  182.1 3.5 slice-start.1
  183.2 2.0 copy-start.2
  185.5 2.4 copy-start.6
  185.8 2.1 copy-start.3
  187.9 6.8 copy-start.13
  210.9 8.1 %copy-start.12 = (f32[768,768]{1,0:T(8,128)S(1)}, f32[768,768]{1,0:T(8,128)}, u32[]{:S(2)}) copy-start(f32[768,768]{1,0:T(8,128)} %fusion.9) | copy-start | bytes 7077892
  220.5 14.0 %slice-start.6 = ((s8[6291456]{0:T(1024)(128)(4,1)}), s8[4194304]{0:T(1024)(128)(4,1)S(1)}, s32[]{:S(2)}) async-start(s8[6291456]{0:T(1024)(128)(4,1)} %bitcast.127), calls=%async_computation.7 | async-start | bytes 8388608
  228.7 5.9 copy-start.10
  228.7 5.9 slice-start.7
  253.1 5.0 copy-start.19
  253.2 5.0 copy-start.20
  253.2 5.0 copy-start.21
  253.2 5.0 copy-start.22
  253.2 48.2 %copy-start.7 = (bf16[768,2304]{1,0:T(8,128)(2,1)S(1)}, bf16[768,2304]{1,0:T(8,128)(2,1)}, u32[]{:S(2)}) copy-start(bf16[768,2304]{1,0:T(8,128)(2,1)} %wqkv_hbm.1) | copy-start | bytes 10616836
Sparse Core Ops, SparseCore 0:
  253.3 432.9 all-reduce.7
